TPU v7x, 32 devices: a whole 2x2x4 slice. The times are simulated.
32 devices in a mesh: gx: 16 (over z, x, core), gy: 2 (over y).
Axes of the slice: x: 2, y: 2, z: 4, core: 2. Of those that a mesh axis runs over, the one named last changes fastest.
Arguments:
- potential: float32 [3, 1, 4096, 256], P(None, None, 'gx', 'gy'), may hold values from -8 to 8
- labels: int32 [1, 4096, 256], P(None, 'gx', 'gy'), may hold values from 0 to 7
- principal: float32 [2, 8], replicated, may hold values from 0.5 to 16
- off_diagonal: float32 [3, 8], replicated, may hold values from -0.4 to 0.4
Outputs:
- updated: float32 [3, 1, 4096, 256], P(None, None, 'gx', 'gy')
All inputs are finite; a program needn't handle non-finite values.
Results may differ from a plain program's by a relative error of at most 0.0017.
Values sent between devices are 32-bit elements; how exact they have to be, the bound alone decides.
A program may use at most 64 MiB of HBM per device.

v0:
```python
import jax
import jax.numpy as jnp
from jax import lax
from jax.sharding import PartitionSpec as P


def shifted_2(shard, axis, by):
    size = lax.axis_size(axis)
    return lax.ppermute(shard, axis, [(i, (i + by) % size) for i in range(size)])


def padded_2(cells, sides, width):
    for axis, dim in sides:
        count = lax.axis_size(axis)
        head = lax.slice_in_dim(cells, 0, width, axis=dim)
        tail = lax.slice_in_dim(cells, cells.shape[dim] - width, cells.shape[dim], axis=dim)
        cells = jnp.concatenate(
            [
                lax.ppermute(tail, axis, [(i, (i + 1) % count) for i in range(count)]),
                cells,
                lax.ppermute(head, axis, [((i + 1) % count, i) for i in range(count)]),
            ],
            axis=dim,
        )
    return cells


def harmonic(first, second):
    return 2.0 * first * second / (first + second)


def neighbour(values, offset, axis_dim, filler):
    extent = values.shape[axis_dim]
    dims_pad = list(values.shape)
    dims_pad[axis_dim] = abs(offset)
    padding = jnp.full(tuple(dims_pad), filler, values.dtype)
    if offset > 0:
        retained = lax.slice_in_dim(values, 0, extent - offset, axis=axis_dim)
        return jnp.concatenate([padding, retained], axis_dim)
    retained = lax.slice_in_dim(values, -offset, extent, axis=axis_dim)
    return jnp.concatenate([retained, padding], axis_dim)


def shifted(values, offset, axis_dim, wrap, filler):
    if wrap:
        return jnp.roll(values, offset, axis_dim)
    return neighbour(values, offset, axis_dim, filler)


def cyclic_reduce(sub_diag, main_diag, super_diag, forcing, axis_dim, wrap):
    extent = sub_diag.shape[axis_dim]
    stride = 1
    while stride < extent:
        low_before = shifted(sub_diag, stride, axis_dim, wrap, 0.0)
        main_before = shifted(main_diag, stride, axis_dim, wrap, 1.0)
        high_before = shifted(super_diag, stride, axis_dim, wrap, 0.0)
        rest_before = shifted(forcing, stride, axis_dim + 1, wrap, 0.0)
        low_after = shifted(sub_diag, -stride, axis_dim, wrap, 0.0)
        main_after = shifted(main_diag, -stride, axis_dim, wrap, 1.0)
        high_after = shifted(super_diag, -stride, axis_dim, wrap, 0.0)
        rest_after = shifted(forcing, -stride, axis_dim + 1, wrap, 0.0)
        factor_low = -sub_diag / main_before
        factor_high = -super_diag / main_after
        forcing = forcing + factor_low[None] * rest_before + factor_high[None] * rest_after
        main_diag = main_diag + factor_low * high_before + factor_high * low_after
        sub_diag = factor_low * low_before
        super_diag = factor_high * high_after
        stride = stride * 2
    return forcing / (sub_diag + main_diag + super_diag)[None]


def reduced_rows(tail_row, next_head, low_last, main_last, high_last, force_last):
    reduced_low = -low_last * tail_row[3]
    reduced_main = main_last - low_last * tail_row[4] - high_last * next_head[3]
    reduced_high = -high_last * next_head[4]
    reduced_force = force_last - low_last[None] * tail_row[:3] - high_last[None] * next_head[:3]
    return jnp.concatenate(
        [reduced_low[None], reduced_main[None], reduced_high[None], reduced_force], 0
    )


def spike_solve(sub_diag, main_diag, super_diag, forcing, axis_dim, interface):
    length = sub_diag.shape[axis_dim]
    position = lax.broadcasted_iota(jnp.int32, sub_diag.shape, axis_dim)
    is_last = position == length - 1
    low_inner = jnp.where((position == 0) | is_last, 0.0, sub_diag)
    high_inner = jnp.where((position == length - 2) | is_last, 0.0, super_diag)
    main_inner = jnp.where(is_last, 1.0, main_diag)
    left_spike = jnp.where(position == 0, sub_diag, 0.0)
    right_spike = jnp.where(position == length - 2, super_diag, 0.0)
    stacked = jnp.concatenate(
        [jnp.where(is_last[None], 0.0, forcing), left_spike[None], right_spike[None]], 0
    )
    solved = cyclic_reduce(low_inner, main_inner, high_inner, stacked, axis_dim, False)
    head_row = lax.slice_in_dim(solved, 0, 1, axis=axis_dim + 1)
    tail_row = lax.slice_in_dim(solved, length - 2, length - 1, axis=axis_dim + 1)
    low_last = lax.slice_in_dim(sub_diag, length - 1, length, axis=axis_dim)
    main_last = lax.slice_in_dim(main_diag, length - 1, length, axis=axis_dim)
    high_last = lax.slice_in_dim(super_diag, length - 1, length, axis=axis_dim)
    force_last = lax.slice_in_dim(forcing, length - 1, length, axis=axis_dim + 1)
    own_value, prev_value = interface(
        head_row, tail_row, low_last, main_last, high_last, force_last
    )
    inner_values = solved[:3] - solved[3][None] * prev_value - solved[4][None] * own_value
    return jnp.where(is_last[None], own_value, inner_values)


def pick_values(solution, members, my_index, axis_dim):
    own_value = lax.dynamic_slice_in_dim(solution, my_index, 1, axis_dim)
    prev_value = lax.dynamic_slice_in_dim(solution, (my_index + members - 1) % members, 1, axis_dim)
    return (own_value, prev_value)


def interface_x(head_row, tail_row, low_last, main_last, high_last, force_last):
    members = lax.axis_size("gx")
    my_index = lax.axis_index("gx")
    next_head = shifted_2(head_row, "gx", -1)
    rows_here = reduced_rows(tail_row, next_head, low_last, main_last, high_last, force_last)
    gathered = lax.all_gather(rows_here, "gx", axis=2, tiled=True)
    solution = cyclic_reduce(gathered[0], gathered[1], gathered[2], gathered[3:], 1, True)
    return pick_values(solution, members, my_index, 2)


def interface_y(head_row, tail_row, low_last, main_last, high_last, force_last):
    members = lax.axis_size("gy")
    next_head = shifted_2(head_row, "gy", -1)
    rows_here = reduced_rows(tail_row, next_head, low_last, main_last, high_last, force_last)
    gathered = lax.all_gather(rows_here, "gy", axis=3, tiled=True)
    solution = cyclic_reduce(gathered[0], gathered[1], gathered[2], gathered[3:], 2, True)
    return pick_values(solution, members, lax.axis_index("gy"), 3)


def lookup_phase(components, label_block):
    cell_tensor = jnp.zeros((5,) + label_block.shape, jnp.float32)
    for phase_id in range(components.shape[1]):
        cell_tensor = jnp.where(
            (label_block == phase_id)[None],
            components[:, phase_id][:, None, None, None],
            cell_tensor,
        )
    return cell_tensor


def local(potential, labels, principal, off_diagonal):
    components = jnp.concatenate([principal, off_diagonal], 0)
    cell_tensor = lookup_phase(components, labels)
    padded = padded_2(cell_tensor, (("gx", 2), ("gy", 3)), 1)
    damping = 2.0 / (potential.shape[3] * potential.shape[3])
    along_xdir = padded[:, :, :, 1:-1]
    cond_xx = along_xdir[0]
    face_east = harmonic(cond_xx[:, 1:-1], cond_xx[:, 2:])
    face_west = harmonic(cond_xx[:, :-2], cond_xx[:, 1:-1])
    source_x = jnp.stack(
        [
            face_east - face_west,
            0.5 * (along_xdir[2][:, 2:] - along_xdir[2][:, :-2]),
            0.5 * (along_xdir[3][:, 2:] - along_xdir[3][:, :-2]),
        ]
    )
    half_step = spike_solve(
        -face_west,
        damping + face_west + face_east,
        -face_east,
        damping * potential + source_x,
        1,
        interface_x,
    )
    along_ydir = padded[:, :, 1:-1, :]
    cond_yy = along_ydir[1]
    face_north = harmonic(cond_yy[:, :, 1:-1], cond_yy[:, :, 2:])
    face_south = harmonic(cond_yy[:, :, :-2], cond_yy[:, :, 1:-1])
    source_y = jnp.stack(
        [
            0.5 * (along_ydir[2][:, :, 2:] - along_ydir[2][:, :, :-2]),
            face_north - face_south,
            0.5 * (along_ydir[4][:, :, 2:] - along_ydir[4][:, :, :-2]),
        ]
    )
    return spike_solve(
        -face_south,
        damping + face_south + face_north,
        -face_north,
        damping * half_step + source_y,
        2,
        interface_y,
    )


def solution(mesh):
    in_specs = (P(None, None, "gx", "gy"), P(None, "gx", "gy"), P(), P())
    out_specs = P(None, None, "gx", "gy")
    return jax.shard_map(local, mesh=mesh, in_specs=in_specs, out_specs=out_specs, check_vma=False)
```

profile of v0, /device:TPU:0, one launch (start us, length us, event | category | flops | bytes accessed | tf_op | source)
XLA Modules:
  0.0 70.5 jit_solution(12789829236502406646)
XLA Ops:
  0.0 0.7 pad_maximum_fusion.15
  0.7 0.3 slice_reduce_fusion.9
  1.0 1.1 %compare_bitcast_fusion.7 = (pred[256,128]{1,0:T(8,128)(4,1)S(1)}, pred[256,128]{1,0:T(8,128)(4,1)S(1)}, pred[256,128]{1,0:T(8,128)(4,1)S(1)}, pred[256,128]{1,0...) fusion(s32[1,256,128]{2,1,0:T(8,128)} %param.5), kind=kLoop, calls=%fused_computation.147 | loop fusion | flops 262144 | bytes 393216 | tf_op jit(solution)/shard_map/jit(_where)/broadcast_in_dim | solution.py:136
  3.1 0.3 select_select_fusion
  3.6 5.5 %collective-permute-start.1 = (f32[5,1,1,128]{2,3,1,0:T(8,128)S(1)}, f32[5,1,1,128]{2,3,1,0:T(8,128)S(1)}, u32[]{:S(2)}, u32[]{:S(2)}) collective-permute-start(f32[5,1,1,128]{2,3,1,0:T(8,128)S(1)} %get-tuple-element.150), channel_id=1, source_target_pairs={{2,0},{4,2},{6,4},{8,6},{10,8},{12,10},{14,12},{16,14},{18,16},{20... | collective-permute-start | bytes 7688 | tf_op jit(solution)/shard_map/ppermute | solution.py:21
  9.0 0.6 iota_compare_fusion.5
  9.6 0.6 fusion.77
  10.2 0.5 iota_compare_fusion.4
  10.7 0.5 iota_compare_fusion.3
  11.2 0.6 fusion.76
  12.1 1.6 %collective-permute-done.1 = f32[5,1,1,128]{2,3,1,0:T(8,128)S(1)} collective-permute-done((f32[5,1,1,128]{2,3,1,0:T(8,128)S(1)}, f32[5,1,1,128]{2,3,1,0:T(8,128)S(1)}, u32[]{:S(2)}, u32[]{:S(2)}) %collective-permute-start.1) | collective-permute-done | bytes 2592 | tf_op jit(solution)/shard_map/ppermute | solution.py:21
  13.6 4.6 %collective-permute-done = f32[5,1,1,128]{2,3,1,0:T(8,128)S(1)} collective-permute-done((f32[5,1,1,128]{2,3,1,0:T(8,128)S(1)}, f32[5,1,1,128]{2,3,1,0:T(8,128)S(1)}, u32[]{:S(2)}, u32[]{:S(2)}) %collective-permute-start) | collective-permute-done | bytes 2592 | tf_op jit(solution)/shard_map/ppermute | solution.py:19
  18.7 0.7 broadcast_select_fusion.3
  20.1 0.3 multiply_add_fusion.12
  21.4 0.3 multiply_add_fusion.11
  22.6 0.3 multiply_add_fusion.10
  28.8 0.7 %pad_maximum_fusion.13 = (f32[5,1,258,1]{2,3,1,0:T(1,128)}, f32[5,1,258,1]{2,3,1,0:T(1,128)}) fusion(f32[5,1,1,128]{2,3,1,0:T(8,128)S(1)} %collective-permute-done.1, f32[5,1,256,128]{2,3,1,0:T(8,128)S(1)} %select_select_fusion, f32[5,1,1,128]{2,3,1,0:T(8,128)S(1)} %collective-permute-done), kind=kLoop, calls=%fused_computation.248 | loop fusion | flops 5160 | bytes 670800 | tf_op jit(solution)/shard_map/slice | solution.py:16
  29.6 1.6 %collective-permute-start.3 = (f32[5,1,258,1]{2,3,1,0:T(1,128)}, f32[5,1,258,1]{2,3,1,0:T(1,128)S(1)}, u32[]{:S(2)}, u32[]{:S(2)}) collective-permute-start(f32[5,1,258,1]{2,3,1,0:T(1,128)} %get-tuple-element.112), channel_id=1, source_target_pairs={{1,0},{0,1},{3,2},{2,3},{5,4},{4,5},{7,6},{6,7},{9,8},{8,9},{11,10... | collective-permute-start | bytes 15488 | tf_op jit(solution)/shard_map/ppermute | solution.py:21
  31.2 0.5 collective-permute-start.2
  31.8 0.6 copy.142
  32.5 0.8 %collective-permute-done.4 = f32[5,1,1,128]{2,3,1,0:T(8,128)S(1)} collective-permute-done((f32[5,1,1,128]{2,3,1,0:T(8,128)S(1)}, f32[5,1,1,128]{2,3,1,0:T(8,128)S(1)}, u32[]{:S(2)}, u32[]{:S(2)}) %collective-permute-start.4) | collective-permute-done | bytes 2592 | tf_op jit(solution)/shard_map/ppermute | solution.py:9
  33.5 0.8 %copy-done.1 = f32[1,256,128]{1,2,0:T(8,128)S(1)} copy-done((f32[1,256,128]{1,2,0:T(8,128)S(1)}, f32[1,256,128]{1,2,0:T(8,128)}, u32[]{:S(2)}) %copy-start.1) | copy-done | bytes 131096
  34.3 0.3 fusion.24
  34.6 0.6 copy-done.2
  35.2 18.7 %all_gather.6 = f32[6,1,16,128]{3,1,0,2:T(1,128)S(1)} all-gather(f32[6,1,1,128]{3,1,0,2:T(1,128)S(1)} %maximum_bitcast_fusion.5), channel_id=1, replica_groups=mesh['gx'=16,'gy'=2] {'gx'}, dimensions={2}, use_global_device_ids=true | all-gather | bytes 52224 | tf_op jit(solution)/shard_map/all_gather | solution.py:119
  55.2 0.7 copy-done.3
  56.0 0.6 copy-done.9
  56.8 0.7 copy-done.5
  61.2 1.6 %collective-permute-start.5 = (f32[5,1,256,1]{2,3,1,0:T(1,128)S(1)}, f32[5,1,256,1]{2,3,1,0:T(1,128)S(1)}, u32[]{:S(2)}, u32[]{:S(2)}) collective-permute-start(f32[5,1,256,1]{2,3,1,0:T(1,128)S(1)} %slice.1303), channel_id=1, source_target_pairs={{0,1},{1,0},{2,3},{3,2},{4,5},{5,4},{6,7},{7,6},{8,9},{9,8},{10,11... | collective-permute-start | bytes 15368 | tf_op jit(solution)/shard_map/ppermute | solution.py:9
  62.8 2.1 %collective-permute-done.5 = f32[5,1,256,1]{2,3,1,0:T(1,128)S(1)} collective-permute-done((f32[5,1,256,1]{2,3,1,0:T(1,128)S(1)}, f32[5,1,256,1]{2,3,1,0:T(1,128)S(1)}, u32[]{:S(2)}, u32[]{:S(2)}) %collective-permute-start.5) | collective-permute-done | bytes 5152 | tf_op jit(solution)/shard_map/ppermute | solution.py:9
  65.0 4.4 %all_gather.7 = f32[6,1,256,2]{2,1,0,3:T(1,128)S(1)} all-gather(f32[6,1,256,1]{2,1,0,3:T(1,128)S(1)} %maximum_bitcast_fusion.4), channel_id=1, replica_groups=mesh['gx'=16,'gy'=2] {'gy'}, dimensions={3}, use_global_device_ids=true | all-gather | bytes 18432 | tf_op jit(solution)/shard_map/all_gather | solution.py:128
  69.6 0.9 %copy.153 = f32[3,1,256,128]{3,2,1,0:T(8,128)} copy(f32[3,1,256,128]{2,3,1,0:T(8,128)S(1)} %fusion.1) | data formatting | bytes 786432 | tf_op jit(solution)/shard_map/jit(_where)/select_n | solution.py:105
  (229 shorter events, 15.1 us)
Async XLA Ops:
  3.4 8.5 %copy-start = (f32[3,1,256,128]{3,2,1,0:T(8,128)S(1)}, f32[3,1,256,128]{3,2,1,0:T(8,128)}, u32[]{:S(2)}) copy-start(f32[3,1,256,128]{3,2,1,0:T(8,128)} %param.4) | copy-start | bytes 1179652
  3.6 10.1 %collective-permute-start.1 = (f32[5,1,1,128]{2,3,1,0:T(8,128)S(1)}, f32[5,1,1,128]{2,3,1,0:T(8,128)S(1)}, u32[]{:S(2)}, u32[]{:S(2)}) collective-permute-start(f32[5,1,1,128]{2,3,1,0:T(8,128)S(1)} %get-tuple-element.150), channel_id=1, source_target_pairs={{2,0},{4,2},{6,4},{8,6},{10,8},{12,10},{14,12},{16,14},{18,16},{20... | collective-permute-start | bytes 7688 | tf_op jit(solution)/shard_map/ppermute | solution.py:21
  9.0 9.2 %collective-permute-start = (f32[5,1,1,128]{2,3,1,0:T(8,128)S(1)}, f32[5,1,1,128]{2,3,1,0:T(8,128)S(1)}, u32[]{:S(2)}, u32[]{:S(2)}) collective-permute-start(f32[5,1,1,128]{2,3,1,0:T(8,128)S(1)} %get-tuple-element.149), channel_id=1, source_target_pairs={{0,2},{2,4},{4,6},{6,8},{8,10},{10,12},{12,14},{14,16},{16,18},{18... | collective-permute-start | bytes 7688 | tf_op jit(solution)/shard_map/ppermute | solution.py:19
  11.8 7.9 %copy-start.4 = (pred[256]{0:T(512)(128)(4,1)}, pred[256]{0:T(512)(128)(4,1)S(1)}, u32[]{:S(2)}) copy-start(pred[256]{0:T(512)(128)(4,1)S(1)} %iota_compare_fusion.2) | copy-start | bytes 772
  28.6 4.8 %collective-permute-start.4 = (f32[5,1,1,128]{2,3,1,0:T(8,128)S(1)}, f32[5,1,1,128]{2,3,1,0:T(8,128)S(1)}, u32[]{:S(2)}, u32[]{:S(2)}) collective-permute-start(f32[5,1,1,128]{2,3,1,0:T(8,128)S(1)} %slice.1169), channel_id=1, source_target_pairs={{0,30},{2,0},{4,2},{6,4},{8,6},{10,8},{12,10},{14,12},{16,14},{18,... | collective-permute-start | bytes 7688 | tf_op jit(solution)/shard_map/ppermute | solution.py:9
  29.6 25.3 %collective-permute-start.3 = (f32[5,1,258,1]{2,3,1,0:T(1,128)}, f32[5,1,258,1]{2,3,1,0:T(1,128)S(1)}, u32[]{:S(2)}, u32[]{:S(2)}) collective-permute-start(f32[5,1,258,1]{2,3,1,0:T(1,128)} %get-tuple-element.112), channel_id=1, source_target_pairs={{1,0},{0,1},{3,2},{2,3},{5,4},{4,5},{7,6},{6,7},{9,8},{8,9},{11,10... | collective-permute-start | bytes 15488 | tf_op jit(solution)/shard_map/ppermute | solution.py:21
  31.2 23.7 %collective-permute-start.2 = (f32[5,1,258,1]{2,3,1,0:T(1,128)}, f32[5,1,258,1]{2,3,1,0:T(1,128)S(1)}, u32[]{:S(2)}, u32[]{:S(2)}) collective-permute-start(f32[5,1,258,1]{2,3,1,0:T(1,128)} %get-tuple-element.111), channel_id=1, source_target_pairs={{0,1},{1,0},{2,3},{3,2},{4,5},{5,4},{6,7},{7,6},{8,9},{9,8},{10,11... | collective-permute-start | bytes 15488 | tf_op jit(solution)/shard_map/ppermute | solution.py:19
  33.4 0.9 %copy-start.1 = (f32[1,256,128]{1,2,0:T(8,128)S(1)}, f32[1,256,128]{1,2,0:T(8,128)}, u32[]{:S(2)}) copy-start(f32[1,256,128]{1,2,0:T(8,128)} %get-tuple-element.102) | copy-start | bytes 393220
  34.6 0.6 copy-start.2
  55.2 0.7 copy-start.3
  55.9 0.7 copy-start.9
  56.0 0.7 copy-start.6
  56.0 0.7 copy-start.7
  56.0 0.6 copy-start.8
  56.8 0.7 copy-start.5
  61.2 3.7 %collective-permute-start.5 = (f32[5,1,256,1]{2,3,1,0:T(1,128)S(1)}, f32[5,1,256,1]{2,3,1,0:T(1,128)S(1)}, u32[]{:S(2)}, u32[]{:S(2)}) collective-permute-start(f32[5,1,256,1]{2,3,1,0:T(1,128)S(1)} %slice.1303), channel_id=1, source_target_pairs={{0,1},{1,0},{2,3},{3,2},{4,5},{5,4},{6,7},{7,6},{8,9},{9,8},{10,11... | collective-permute-start | bytes 15368 | tf_op jit(solution)/shard_map/ppermute | solution.py:9
where the time goes:
time: 70.8 us; the launch traced here: 70.5 us
  blocking collectives  23.1 us (33%)
  other arithmetic  15.5 us (22%)
  local copies, waits for them, and re-layouts  12 us (17%)
  starting transfers between devices  9.31 us (13%)
  waiting for transfers between devices  9.1 us (13%)
  between operations  1.55 us (2%)
    all_gather x1, blocking collectives, interface_x(): gathered = lax.all_gather(rows_here, 'gx', axis=2, tiled=True)  18.7 us
    ppermute x2, starting transfers between devices, padded_2(): lax.ppermute(head, axis, [((i + 1) % count, i) for i in range(count)])  7.05 us
    ppermute x2, waiting for transfers between devices, padded_2(): lax.ppermute(tail, axis, [(i, (i + 1) % count) for i in range(count)])  4.61 us
    all_gather x1, blocking collectives, interface_y(): gathered = lax.all_gather(rows_here, 'gy', axis=3, tiled=True)  4.36 us
    slice x47, local copies, waits for them, and re-layouts, neighbour(): retained = lax.slice_in_dim(values, 0, extent - offset, axis=axis_dim)  3.91 us
    unnamed x28, local copies, waits for them, and re-layouts  3.57 us
    add x16, other arithmetic, cyclic_reduce(): forcing + factor_low[None] * rest_before + factor_high[None] * rest_after  3.03 us
    ppermute x2, waiting for transfers between devices, shifted_2(): lax.ppermute(shard, axis, [(i, (i + by) % size) for i in range(size)])  2.92 us
  transfers between devices with their start and end apart: 6, of which 4 were waited for; matrix products, arithmetic and copies ran while one was open for 8% of the time, Pallas kernels for 0%

commit v1 on v0

--- a/solution.py
+++ b/solution.py
@@ -2,6 +2,16 @@
 import jax.numpy as jnp
 from jax import lax
 from jax.sharding import PartitionSpec as P
+
+
+def pass_along(x, axis, dim):
+    count = lax.axis_size(axis)
+    current, shards = (x, [x])
+    for _ in range(count - 1):
+        current = lax.ppermute(current, axis, [(i, (i + 1) % count) for i in range(count)])
+        shards.insert(0, current)
+    flat = jnp.concatenate(shards, axis=dim)
+    return jnp.roll(flat, (lax.axis_index(axis) + 1) * x.shape[dim], axis=dim)
 
 
 def shifted_2(shard, axis, by):
@@ -116,7 +126,7 @@
     my_index = lax.axis_index("gx")
     next_head = shifted_2(head_row, "gx", -1)
     rows_here = reduced_rows(tail_row, next_head, low_last, main_last, high_last, force_last)
-    gathered = lax.all_gather(rows_here, "gx", axis=2, tiled=True)
+    gathered = pass_along(rows_here, "gx", 2)
     solution = cyclic_reduce(gathered[0], gathered[1], gathered[2], gathered[3:], 1, True)
     return pick_values(solution, members, my_index, 2)
 

time: 70.8 us -> 142 us (2.01)
  waiting for transfers between devices: 9.1 us -> 84.2 us
  blocking collectives: 23.1 us -> 4.36 us
  local copies, waits for them, and re-layouts: 12 us -> 23.9 us
  other arithmetic: 15.5 us -> 17.8 us
    ppermute x0 -> x15, waiting for transfers between devices: none -> 74 us  [pass_along(): lax.ppermute(current, axis, [(i, (i + 1) % count) for i in range(count)])]
    all_gather x1 -> x0, blocking collectives: 18.7 us -> none  [interface_x(): gathered = lax.all_gather(rows_here, 'gx', axis=2, tiled=True)]
    unnamed x28 -> x52, local copies, waits for them, and re-layouts: 3.57 us -> 9.86 us
    concatenate x0 -> x1, local copies, waits for them, and re-layouts: none -> 5.39 us  [pass_along(): return jnp.roll(flat, (lax.axis_index(axis) + 1) * x.shape[dim], axis=dim)]
  transfers between devices with their start and end apart: 6 -> 21, of which waited for: 4 -> 20; matrix products, arithmetic and copies ran while one was open for 8% -> 6% of each run, Pallas kernels for 0% -> 0%
where the time goes in v1:
time: 142 us; the launch traced here: 141 us
  waiting for transfers between devices  84.2 us (59%)
  local copies, waits for them, and re-layouts  23.9 us (17%)
  other arithmetic  17.8 us (13%)
  starting transfers between devices  9.41 us (7%)
  blocking collectives  4.36 us (3%)
  between operations  1.55 us (1%)
    ppermute x15, waiting for transfers between devices, pass_along(): lax.ppermute(current, axis, [(i, (i + 1) % count) for i in range(count)])  74 us
    unnamed x52, local copies, waits for them, and re-layouts  9.86 us
    ppermute x2, starting transfers between devices, padded_2(): lax.ppermute(head, axis, [((i + 1) % count, i) for i in range(count)])  7.05 us
    concatenate x1, local copies, waits for them, and re-layouts, pass_along(): return jnp.roll(flat, (lax.axis_index(axis) + 1) * x.shape[dim], axis=dim)  5.39 us
    ppermute x2, waiting for transfers between devices, padded_2(): lax.ppermute(tail, axis, [(i, (i + 1) % count) for i in range(count)])  5.05 us
    all_gather x1, blocking collectives, interface_y(): gathered = lax.all_gather(rows_here, 'gy', axis=3, tiled=True)  4.36 us
    slice x47, local copies, waits for them, and re-layouts, neighbour(): retained = lax.slice_in_dim(values, 0, extent - offset, axis=axis_dim)  3.94 us
    ppermute x2, waiting for transfers between devices, shifted_2(): lax.ppermute(shard, axis, [(i, (i + by) % size) for i in range(size)])  3.43 us
  transfers between devices with their start and end apart: 21, of which 20 were waited for; matrix products, arithmetic and copies ran while one was open for 6% of the time, Pallas kernels for 0%

profile of v1, /device:TPU:0, one launch (start us, length us, event | category | flops | bytes accessed | tf_op | source)
XLA Modules:
  0.0 141.2 jit_solution(3635747334085594509)
XLA Ops:
  1.0 1.1 compare_bitcast_fusion.7
  3.6 5.5 %collective-permute-start.1 = (f32[5,1,1,128]{2,3,1,0:T(8,128)S(1)}, f32[5,1,1,128]{2,3,1,0:T(8,128)S(1)}, u32[]{:S(2)}, u32[]{:S(2)}) collective-permute-start(f32[5,1,1,128]{2,3,1,0:T(8,128)S(1)} %get-tuple-element.150), channel_id=1, source_target_pairs={{2,0},{4,2},{6,4},{8,6},{10,8},{12,10},{14,12},{16,14},{18,16},{20... | collective-permute-start | bytes 7688 | tf_op jit(solution)/shard_map/ppermute | solution.py:31
  12.0 1.7 %collective-permute-done.1 = f32[5,1,1,128]{2,3,1,0:T(8,128)S(1)} collective-permute-done((f32[5,1,1,128]{2,3,1,0:T(8,128)S(1)}, f32[5,1,1,128]{2,3,1,0:T(8,128)S(1)}, u32[]{:S(2)}, u32[]{:S(2)}) %collective-permute-start.1) | collective-permute-done | bytes 2592 | tf_op jit(solution)/shard_map/ppermute | solution.py:31
  13.6 4.6 %collective-permute-done = f32[5,1,1,128]{2,3,1,0:T(8,128)S(1)} collective-permute-done((f32[5,1,1,128]{2,3,1,0:T(8,128)S(1)}, f32[5,1,1,128]{2,3,1,0:T(8,128)S(1)}, u32[]{:S(2)}, u32[]{:S(2)}) %collective-permute-start) | collective-permute-done | bytes 2592 | tf_op jit(solution)/shard_map/ppermute | solution.py:29
  28.8 0.7 pad_maximum_fusion.13
  29.6 1.6 %collective-permute-start.3 = (f32[5,1,258,1]{2,3,1,0:T(1,128)}, f32[5,1,258,1]{2,3,1,0:T(1,128)S(1)}, u32[]{:S(2)}, u32[]{:S(2)}) collective-permute-start(f32[5,1,258,1]{2,3,1,0:T(1,128)} %get-tuple-element.112), channel_id=1, source_target_pairs={{1,0},{0,1},{3,2},{2,3},{5,4},{4,5},{7,6},{6,7},{9,8},{8,9},{11,10... | collective-permute-start | bytes 15488 | tf_op jit(solution)/shard_map/ppermute | solution.py:31
  32.0 1.4 collective-permute-done.4
  33.5 0.8 copy-done.2
  35.1 0.8 maximum_bitcast_fusion.2
  36.0 0.8 fusion.108
  40.6 5.7 %collective-permute-done.6 = f32[6,1,1,128]{3,2,1,0:T(1,128)S(1)} collective-permute-done((f32[6,1,1,128]{3,2,1,0:T(1,128)S(1)}, f32[6,1,1,128]{3,2,1,0:T(1,128)S(1)}, u32[]{:S(2)}, u32[]{:S(2)}) %collective-permute-start.6) | collective-permute-done | bytes 3104 | tf_op jit(solution)/shard_map/ppermute | solution.py:11
  46.3 5.7 %collective-permute-done.7 = f32[6,1,1,128]{3,2,1,0:T(1,128)S(1)} collective-permute-done((f32[6,1,1,128]{3,2,1,0:T(1,128)S(1)}, f32[6,1,1,128]{3,2,1,0:T(1,128)S(1)}, u32[]{:S(2)}, u32[]{:S(2)}) %collective-permute-start.7) | collective-permute-done | bytes 3104 | tf_op jit(solution)/shard_map/ppermute | solution.py:11
  52.1 5.7 %collective-permute-done.8 = f32[6,1,1,128]{3,2,1,0:T(1,128)S(1)} collective-permute-done((f32[6,1,1,128]{3,2,1,0:T(1,128)S(1)}, f32[6,1,1,128]{3,2,1,0:T(1,128)S(1)}, u32[]{:S(2)}, u32[]{:S(2)}) %collective-permute-start.8) | collective-permute-done | bytes 3104 | tf_op jit(solution)/shard_map/ppermute | solution.py:11
  58.3 5.1 %collective-permute-done.9 = f32[6,1,1,128]{3,2,1,0:T(1,128)S(1)} collective-permute-done((f32[6,1,1,128]{3,2,1,0:T(1,128)S(1)}, f32[6,1,1,128]{3,2,1,0:T(1,128)S(1)}, u32[]{:S(2)}, u32[]{:S(2)}) %collective-permute-start.9) | collective-permute-done | bytes 3104 | tf_op jit(solution)/shard_map/ppermute | solution.py:11
  64.0 5.1 %collective-permute-done.10 = f32[6,1,1,128]{3,2,1,0:T(1,128)S(1)} collective-permute-done((f32[6,1,1,128]{3,2,1,0:T(1,128)S(1)}, f32[6,1,1,128]{3,2,1,0:T(1,128)S(1)}, u32[]{:S(2)}, u32[]{:S(2)}) %collective-permute-start.10) | collective-permute-done | bytes 3104 | tf_op jit(solution)/shard_map/ppermute | solution.py:11
  69.8 5.1 %collective-permute-done.11 = f32[6,1,1,128]{3,2,1,0:T(1,128)S(1)} collective-permute-done((f32[6,1,1,128]{3,2,1,0:T(1,128)S(1)}, f32[6,1,1,128]{3,2,1,0:T(1,128)S(1)}, u32[]{:S(2)}, u32[]{:S(2)}) %collective-permute-start.11) | collective-permute-done | bytes 3104 | tf_op jit(solution)/shard_map/ppermute | solution.py:11
  75.5 5.1 %collective-permute-done.12 = f32[6,1,1,128]{3,2,1,0:T(1,128)S(1)} collective-permute-done((f32[6,1,1,128]{3,2,1,0:T(1,128)S(1)}, f32[6,1,1,128]{3,2,1,0:T(1,128)S(1)}, u32[]{:S(2)}, u32[]{:S(2)}) %collective-permute-start.12) | collective-permute-done | bytes 3104 | tf_op jit(solution)/shard_map/ppermute | solution.py:11
  81.2 5.1 %collective-permute-done.13 = f32[6,1,1,128]{3,2,1,0:T(1,128)S(1)} collective-permute-done((f32[6,1,1,128]{3,2,1,0:T(1,128)S(1)}, f32[6,1,1,128]{3,2,1,0:T(1,128)S(1)}, u32[]{:S(2)}, u32[]{:S(2)}) %collective-permute-start.13) | collective-permute-done | bytes 3104 | tf_op jit(solution)/shard_map/ppermute | solution.py:11
  86.9 5.1 %collective-permute-done.14 = f32[6,1,1,128]{3,2,1,0:T(1,128)S(1)} collective-permute-done((f32[6,1,1,128]{3,2,1,0:T(1,128)S(1)}, f32[6,1,1,128]{3,2,1,0:T(1,128)S(1)}, u32[]{:S(2)}, u32[]{:S(2)}) %collective-permute-start.14) | collective-permute-done | bytes 3104 | tf_op jit(solution)/shard_map/ppermute | solution.py:11
  92.6 5.1 %collective-permute-done.15 = f32[6,1,1,128]{3,2,1,0:T(1,128)S(1)} collective-permute-done((f32[6,1,1,128]{3,2,1,0:T(1,128)S(1)}, f32[6,1,1,128]{3,2,1,0:T(1,128)S(1)}, u32[]{:S(2)}, u32[]{:S(2)}) %collective-permute-start.15) | collective-permute-done | bytes 3104 | tf_op jit(solution)/shard_map/ppermute | solution.py:11
  98.4 5.1 %collective-permute-done.16 = f32[6,1,1,128]{3,2,1,0:T(1,128)S(1)} collective-permute-done((f32[6,1,1,128]{3,2,1,0:T(1,128)S(1)}, f32[6,1,1,128]{3,2,1,0:T(1,128)S(1)}, u32[]{:S(2)}, u32[]{:S(2)}) %collective-permute-start.16) | collective-permute-done | bytes 3104 | tf_op jit(solution)/shard_map/ppermute | solution.py:11
  104.1 5.1 %collective-permute-done.17 = f32[6,1,1,128]{3,2,1,0:T(1,128)S(1)} collective-permute-done((f32[6,1,1,128]{3,2,1,0:T(1,128)S(1)}, f32[6,1,1,128]{3,2,1,0:T(1,128)S(1)}, u32[]{:S(2)}, u32[]{:S(2)}) %collective-permute-start.17) | collective-permute-done | bytes 3104 | tf_op jit(solution)/shard_map/ppermute | solution.py:11
  109.8 5.1 %collective-permute-done.18 = f32[6,1,1,128]{3,2,1,0:T(1,128)S(1)} collective-permute-done((f32[6,1,1,128]{3,2,1,0:T(1,128)S(1)}, f32[6,1,1,128]{3,2,1,0:T(1,128)S(1)}, u32[]{:S(2)}, u32[]{:S(2)}) %collective-permute-start.18) | collective-permute-done | bytes 3104 | tf_op jit(solution)/shard_map/ppermute | solution.py:11
  115.5 5.2 %collective-permute-done.19 = f32[6,1,1,128]{3,2,1,0:T(1,128)} collective-permute-done((f32[6,1,1,128]{3,2,1,0:T(1,128)S(1)}, f32[6,1,1,128]{3,2,1,0:T(1,128)}, u32[]{:S(2)}, u32[]{:S(2)}) %collective-permute-start.19) | collective-permute-done | bytes 3104 | tf_op jit(solution)/shard_map/ppermute | solution.py:11
  120.8 5.4 %concatenate.1220 = f32[6,1,32,128]{3,2,1,0:T(8,128)} concatenate(f32[6,1,1,128]{3,2,1,0:T(1,128)} %collective-permute-done.19, f32[6,1,1,128]{3,2,1,0:T(1,128)} %copy-done.13, f32[6,1,1,128]{3,2,1,0:T(1,128)} %copy-done.12, f32[6,1,1,128]{3,2,1,0:T(1,128)} %copy-done.11, f32[6,1,1,128]{3,2,1,0:T(1,128)} %copy-done.10, f32[6,1,1,128]{3,2,1,0:T(1,128)} %copy-done.9, ...), dimensions={2} | concatenate | bytes 196608 | tf_op jit(solution)/shard_map/jit(_roll_dynamic)/concatenate | solution.py:14
  126.1 0.7 dynamic-slice_bitcast_fusion
  127.2 0.8 copy-done
  131.2 1.6 %collective-permute-start.20 = (f32[5,1,256,1]{2,3,1,0:T(1,128)S(1)}, f32[5,1,256,1]{2,3,1,0:T(1,128)S(1)}, u32[]{:S(2)}, u32[]{:S(2)}) collective-permute-start(f32[5,1,256,1]{2,3,1,0:T(1,128)S(1)} %slice.1295), channel_id=1, source_target_pairs={{0,1},{1,0},{2,3},{3,2},{4,5},{5,4},{6,7},{7,6},{8,9},{9,8},{10,11... | collective-permute-start | bytes 15368 | tf_op jit(solution)/shard_map/ppermute | solution.py:19
  132.8 2.1 %collective-permute-done.20 = f32[5,1,256,1]{2,3,1,0:T(1,128)S(1)} collective-permute-done((f32[5,1,256,1]{2,3,1,0:T(1,128)S(1)}, f32[5,1,256,1]{2,3,1,0:T(1,128)S(1)}, u32[]{:S(2)}, u32[]{:S(2)}) %collective-permute-start.20) | collective-permute-done | bytes 5152 | tf_op jit(solution)/shard_map/ppermute | solution.py:19
  134.9 0.7 fusion.74
  135.6 4.4 %all_gather.3 = f32[6,1,256,2]{2,1,0,3:T(1,128)S(1)} all-gather(f32[6,1,256,1]{2,1,0,3:T(1,128)S(1)} %maximum_bitcast_fusion.4), channel_id=1, replica_groups=mesh['gx'=16,'gy'=2] {'gy'}, dimensions={3}, use_global_device_ids=true | all-gather | bytes 18432 | tf_op jit(solution)/shard_map/all_gather | solution.py:138
  140.3 0.9 copy.141
  (283 shorter events, 30.6 us)
Async XLA Ops:
  3.4 8.3 %copy-start.1 = (f32[3,1,256,128]{3,2,1,0:T(8,128)S(1)}, f32[3,1,256,128]{3,2,1,0:T(8,128)}, u32[]{:S(2)}) copy-start(f32[3,1,256,128]{3,2,1,0:T(8,128)} %param.4) | copy-start | bytes 1179652
  3.6 10.1 %collective-permute-start.1 = (f32[5,1,1,128]{2,3,1,0:T(8,128)S(1)}, f32[5,1,1,128]{2,3,1,0:T(8,128)S(1)}, u32[]{:S(2)}, u32[]{:S(2)}) collective-permute-start(f32[5,1,1,128]{2,3,1,0:T(8,128)S(1)} %get-tuple-element.150), channel_id=1, source_target_pairs={{2,0},{4,2},{6,4},{8,6},{10,8},{12,10},{14,12},{16,14},{18,16},{20... | collective-permute-start | bytes 7688 | tf_op jit(solution)/shard_map/ppermute | solution.py:31
  9.0 9.2 %collective-permute-start = (f32[5,1,1,128]{2,3,1,0:T(8,128)S(1)}, f32[5,1,1,128]{2,3,1,0:T(8,128)S(1)}, u32[]{:S(2)}, u32[]{:S(2)}) collective-permute-start(f32[5,1,1,128]{2,3,1,0:T(8,128)S(1)} %get-tuple-element.149), channel_id=1, source_target_pairs={{0,2},{2,4},{4,6},{6,8},{8,10},{10,12},{12,14},{14,16},{16,18},{18... | collective-permute-start | bytes 7688 | tf_op jit(solution)/shard_map/ppermute | solution.py:29
  11.7 8.1 %copy-start.16 = (pred[256]{0:T(512)(128)(4,1)}, pred[256]{0:T(512)(128)(4,1)S(1)}, u32[]{:S(2)}) copy-start(pred[256]{0:T(512)(128)(4,1)S(1)} %iota_compare_fusion.2) | copy-start | bytes 772
  28.6 4.8 %collective-permute-start.4 = (f32[5,1,1,128]{2,3,1,0:T(8,128)S(1)}, f32[5,1,1,128]{2,3,1,0:T(8,128)S(1)}, u32[]{:S(2)}, u32[]{:S(2)}) collective-permute-start(f32[5,1,1,128]{2,3,1,0:T(8,128)S(1)} %slice.1169), channel_id=1, source_target_pairs={{0,30},{2,0},{4,2},{6,4},{8,6},{10,8},{12,10},{14,12},{16,14},{18,... | collective-permute-start | bytes 7688 | tf_op jit(solution)/shard_map/ppermute | solution.py:19
  29.6 5.1 %collective-permute-start.3 = (f32[5,1,258,1]{2,3,1,0:T(1,128)}, f32[5,1,258,1]{2,3,1,0:T(1,128)S(1)}, u32[]{:S(2)}, u32[]{:S(2)}) collective-permute-start(f32[5,1,258,1]{2,3,1,0:T(1,128)} %get-tuple-element.112), channel_id=1, source_target_pairs={{1,0},{0,1},{3,2},{2,3},{5,4},{4,5},{7,6},{6,7},{9,8},{8,9},{11,10... | collective-permute-start | bytes 15488 | tf_op jit(solution)/shard_map/ppermute | solution.py:31
  31.2 4.0 %collective-permute-start.2 = (f32[5,1,258,1]{2,3,1,0:T(1,128)}, f32[5,1,258,1]{2,3,1,0:T(1,128)}, u32[]{:S(2)}, u32[]{:S(2)}) collective-permute-start(f32[5,1,258,1]{2,3,1,0:T(1,128)} %get-tuple-element.111), channel_id=1, source_target_pairs={{0,1},{1,0},{2,3},{3,2},{4,5},{5,4},{6,7},{7,6},{8,9},{9,8},{10,11... | collective-permute-start | bytes 15488 | tf_op jit(solution)/shard_map/ppermute | solution.py:29
  33.4 0.9 copy-start.2
  34.6 5.9 %collective-permute-start.5 = (f32[6,1,1,128]{3,2,1,0:T(1,128)S(1)}, f32[6,1,1,128]{3,2,1,0:T(1,128)S(1)}, u32[]{:S(2)}, u32[]{:S(2)}) collective-permute-start(f32[6,1,1,128]{3,2,1,0:T(1,128)S(1)} %pad_maximum_fusion.16), channel_id=1, source_target_pairs={{0,2},{2,4},{4,6},{6,8},{8,10},{10,12},{12,14},{14,16},{16,18},{18... | collective-permute-start | bytes 9224 | tf_op jit(solution)/shard_map/ppermute | solution.py:11
  36.7 0.7 copy-start.14
  37.4 0.7 copy-start.21
  38.1 0.6 copy-start.18
  38.1 0.6 copy-start.19
  38.1 0.6 copy-start.20
  40.6 5.7 %collective-permute-start.6 = (f32[6,1,1,128]{3,2,1,0:T(1,128)S(1)}, f32[6,1,1,128]{3,2,1,0:T(1,128)S(1)}, u32[]{:S(2)}, u32[]{:S(2)}) collective-permute-start(f32[6,1,1,128]{3,2,1,0:T(1,128)S(1)} %collective-permute-done.5), channel_id=1, source_target_pairs={{0,2},{2,4},{4,6},{6,8},{8,10},{10,12},{12,14},{14,16},{16,18},{18... | collective-permute-start | bytes 9224 | tf_op jit(solution)/shard_map/ppermute | solution.py:11
  46.3 5.7 %collective-permute-start.7 = (f32[6,1,1,128]{3,2,1,0:T(1,128)S(1)}, f32[6,1,1,128]{3,2,1,0:T(1,128)S(1)}, u32[]{:S(2)}, u32[]{:S(2)}) collective-permute-start(f32[6,1,1,128]{3,2,1,0:T(1,128)S(1)} %collective-permute-done.6), channel_id=1, source_target_pairs={{0,2},{2,4},{4,6},{6,8},{8,10},{10,12},{12,14},{14,16},{16,18},{18... | collective-permute-start | bytes 9224 | tf_op jit(solution)/shard_map/ppermute | solution.py:11
  52.0 5.7 %collective-permute-start.8 = (f32[6,1,1,128]{3,2,1,0:T(1,128)S(1)}, f32[6,1,1,128]{3,2,1,0:T(1,128)S(1)}, u32[]{:S(2)}, u32[]{:S(2)}) collective-permute-start(f32[6,1,1,128]{3,2,1,0:T(1,128)S(1)} %collective-permute-done.7), channel_id=1, source_target_pairs={{0,2},{2,4},{4,6},{6,8},{8,10},{10,12},{12,14},{14,16},{16,18},{18... | collective-permute-start | bytes 9224 | tf_op jit(solution)/shard_map/ppermute | solution.py:11
  57.7 5.7 %collective-permute-start.9 = (f32[6,1,1,128]{3,2,1,0:T(1,128)S(1)}, f32[6,1,1,128]{3,2,1,0:T(1,128)S(1)}, u32[]{:S(2)}, u32[]{:S(2)}) collective-permute-start(f32[6,1,1,128]{3,2,1,0:T(1,128)S(1)} %collective-permute-done.8), channel_id=1, source_target_pairs={{0,2},{2,4},{4,6},{6,8},{8,10},{10,12},{12,14},{14,16},{16,18},{18... | collective-permute-start | bytes 9224 | tf_op jit(solution)/shard_map/ppermute | solution.py:11
  63.4 5.7 %collective-permute-start.10 = (f32[6,1,1,128]{3,2,1,0:T(1,128)S(1)}, f32[6,1,1,128]{3,2,1,0:T(1,128)S(1)}, u32[]{:S(2)}, u32[]{:S(2)}) collective-permute-start(f32[6,1,1,128]{3,2,1,0:T(1,128)S(1)} %collective-permute-done.9), channel_id=1, source_target_pairs={{0,2},{2,4},{4,6},{6,8},{8,10},{10,12},{12,14},{14,16},{16,18},{18... | collective-permute-start | bytes 9224 | tf_op jit(solution)/shard_map/ppermute | solution.py:11
  69.2 5.7 %collective-permute-start.11 = (f32[6,1,1,128]{3,2,1,0:T(1,128)S(1)}, f32[6,1,1,128]{3,2,1,0:T(1,128)S(1)}, u32[]{:S(2)}, u32[]{:S(2)}) collective-permute-start(f32[6,1,1,128]{3,2,1,0:T(1,128)S(1)} %collective-permute-done.10), channel_id=1, source_target_pairs={{0,2},{2,4},{4,6},{6,8},{8,10},{10,12},{12,14},{14,16},{16,18},{18... | collective-permute-start | bytes 9224 | tf_op jit(solution)/shard_map/ppermute | solution.py:11
  74.9 5.7 %collective-permute-start.12 = (f32[6,1,1,128]{3,2,1,0:T(1,128)S(1)}, f32[6,1,1,128]{3,2,1,0:T(1,128)S(1)}, u32[]{:S(2)}, u32[]{:S(2)}) collective-permute-start(f32[6,1,1,128]{3,2,1,0:T(1,128)S(1)} %collective-permute-done.11), channel_id=1, source_target_pairs={{0,2},{2,4},{4,6},{6,8},{8,10},{10,12},{12,14},{14,16},{16,18},{18... | collective-permute-start | bytes 9224 | tf_op jit(solution)/shard_map/ppermute | solution.py:11
  80.6 5.7 %collective-permute-start.13 = (f32[6,1,1,128]{3,2,1,0:T(1,128)S(1)}, f32[6,1,1,128]{3,2,1,0:T(1,128)S(1)}, u32[]{:S(2)}, u32[]{:S(2)}) collective-permute-start(f32[6,1,1,128]{3,2,1,0:T(1,128)S(1)} %collective-permute-done.12), channel_id=1, source_target_pairs={{0,2},{2,4},{4,6},{6,8},{8,10},{10,12},{12,14},{14,16},{16,18},{18... | collective-permute-start | bytes 9224 | tf_op jit(solution)/shard_map/ppermute | solution.py:11
  86.3 5.7 %collective-permute-start.14 = (f32[6,1,1,128]{3,2,1,0:T(1,128)S(1)}, f32[6,1,1,128]{3,2,1,0:T(1,128)S(1)}, u32[]{:S(2)}, u32[]{:S(2)}) collective-permute-start(f32[6,1,1,128]{3,2,1,0:T(1,128)S(1)} %collective-permute-done.13), channel_id=1, source_target_pairs={{0,2},{2,4},{4,6},{6,8},{8,10},{10,12},{12,14},{14,16},{16,18},{18... | collective-permute-start | bytes 9224 | tf_op jit(solution)/shard_map/ppermute | solution.py:11
  92.0 5.7 %collective-permute-start.15 = (f32[6,1,1,128]{3,2,1,0:T(1,128)S(1)}, f32[6,1,1,128]{3,2,1,0:T(1,128)S(1)}, u32[]{:S(2)}, u32[]{:S(2)}) collective-permute-start(f32[6,1,1,128]{3,2,1,0:T(1,128)S(1)} %collective-permute-done.14), channel_id=1, source_target_pairs={{0,2},{2,4},{4,6},{6,8},{8,10},{10,12},{12,14},{14,16},{16,18},{18... | collective-permute-start | bytes 9224 | tf_op jit(solution)/shard_map/ppermute | solution.py:11
  97.8 5.7 %collective-permute-start.16 = (f32[6,1,1,128]{3,2,1,0:T(1,128)S(1)}, f32[6,1,1,128]{3,2,1,0:T(1,128)S(1)}, u32[]{:S(2)}, u32[]{:S(2)}) collective-permute-start(f32[6,1,1,128]{3,2,1,0:T(1,128)S(1)} %collective-permute-done.15), channel_id=1, source_target_pairs={{0,2},{2,4},{4,6},{6,8},{8,10},{10,12},{12,14},{14,16},{16,18},{18... | collective-permute-start | bytes 9224 | tf_op jit(solution)/shard_map/ppermute | solution.py:11
  103.5 5.7 %collective-permute-start.17 = (f32[6,1,1,128]{3,2,1,0:T(1,128)S(1)}, f32[6,1,1,128]{3,2,1,0:T(1,128)S(1)}, u32[]{:S(2)}, u32[]{:S(2)}) collective-permute-start(f32[6,1,1,128]{3,2,1,0:T(1,128)S(1)} %collective-permute-done.16), channel_id=1, source_target_pairs={{0,2},{2,4},{4,6},{6,8},{8,10},{10,12},{12,14},{14,16},{16,18},{18... | collective-permute-start | bytes 9224 | tf_op jit(solution)/shard_map/ppermute | solution.py:11
  109.2 5.7 %collective-permute-start.18 = (f32[6,1,1,128]{3,2,1,0:T(1,128)S(1)}, f32[6,1,1,128]{3,2,1,0:T(1,128)S(1)}, u32[]{:S(2)}, u32[]{:S(2)}) collective-permute-start(f32[6,1,1,128]{3,2,1,0:T(1,128)S(1)} %collective-permute-done.17), channel_id=1, source_target_pairs={{0,2},{2,4},{4,6},{6,8},{8,10},{10,12},{12,14},{14,16},{16,18},{18... | collective-permute-start | bytes 9224 | tf_op jit(solution)/shard_map/ppermute | solution.py:11
  114.9 5.8 %collective-permute-start.19 = (f32[6,1,1,128]{3,2,1,0:T(1,128)S(1)}, f32[6,1,1,128]{3,2,1,0:T(1,128)}, u32[]{:S(2)}, u32[]{:S(2)}) collective-permute-start(f32[6,1,1,128]{3,2,1,0:T(1,128)S(1)} %collective-permute-done.18), channel_id=1, source_target_pairs={{0,2},{2,4},{4,6},{6,8},{8,10},{10,12},{12,14},{14,16},{16,18},{18... | collective-permute-start | bytes 9224 | tf_op jit(solution)/shard_map/ppermute | solution.py:11
  127.1 0.9 copy-start
  128.4 0.7 copy-start.15
  128.4 0.7 copy-start.17
  131.2 3.7 %collective-permute-start.20 = (f32[5,1,256,1]{2,3,1,0:T(1,128)S(1)}, f32[5,1,256,1]{2,3,1,0:T(1,128)S(1)}, u32[]{:S(2)}, u32[]{:S(2)}) collective-permute-start(f32[5,1,256,1]{2,3,1,0:T(1,128)S(1)} %slice.1295), channel_id=1, source_target_pairs={{0,1},{1,0},{2,3},{3,2},{4,5},{5,4},{6,7},{7,6},{8,9},{9,8},{10,11... | collective-permute-start | bytes 15368 | tf_op jit(solution)/shard_map/ppermute | solution.py:19
  (11 other events, 6.4 us)
